TPU v7x, 512 devices: a whole 4x8x8 slice. The times are simulated.
512 devices in a mesh: pb: 32 (over z_hi, y, core), dev: 16 (over x, z_lo).
Axes of the slice: x: 4, y: 8, z: 8 (z_hi: 2, z_lo: 4; z = z_hi * 4 + z_lo), core: 2. Of those that a mesh axis runs over, the one named last changes fastest.
Arguments:
- query_factors: float32 [32768, 128], P('pb'), may hold values from -2.4 to 2.4
- panel_factors: float32 [131072, 128], P(('pb', 'dev')), may hold values from -2.4 to 2.4
- query_weight: float32 [32768], P('pb'), may hold values from 1 to 144, as said below
- plan: int32 [32], replicated, may hold values from 0 to 31, each once
- tile_seeds: int32 [32, 32], replicated, may hold values from 0 to 65520
Outputs:
- query_out: float32 [32768, 128], P('pb')
- panel_out: float32 [131072, 128], P(('pb', 'dev'))
Inputs may be any that keep to these rules, and one draw needn't show every extreme that they name: `query_weight`: each row's weight is positive and at most 144.
All inputs are finite; a program needn't handle non-finite values.
Results may differ from a plain program's by a relative error of at most 0.00018.
Values sent between devices are 32-bit elements; how exact they have to be, the bound alone decides.
A program may use at most 64 MiB of HBM per device.

v0:
```python
import jax
import jax.numpy as jnp
from jax import lax
from jax.sharding import Mesh
from jax.sharding import PartitionSpec as P

STRATA = 3
PB = ("pb_0", "pb_1", "pb_2")
DEV = ("dev_0", "dev_1")
PB_DEV = ("pb_0", "pb_1", "pb_2", "dev_0", "dev_1")


epsilon = 1e-06
learning_rate = 0.3


def in_blocks(array, dim, size):
    before, after = (array.shape[:dim], array.shape[dim + 1 :])
    return jnp.moveaxis(array.reshape(*before, size, -1, *after), dim, 0)


def sent_and_summed(array, axis, dim):
    size = lax.axis_size(axis)
    parts = lax.all_to_all(in_blocks(array, dim, size), axis, 0, 0, tiled=True)
    return jnp.sum(parts, axis=0)


def one_axis_at_a_time(array, axes):
    for axis in axes:
        array = lax.psum(array, axis)
    return array


def sent_to_all(array, axis):
    copies = jnp.broadcast_to(array, (lax.axis_size(axis), *array.shape))
    return lax.all_to_all(copies, axis, split_axis=0, concat_axis=0, tiled=True)


def laid_out(parts, dim):
    parts = jnp.moveaxis(parts, 0, dim)
    shape = parts.shape
    return parts.reshape(*shape[:dim], shape[dim] * shape[dim + 1], *shape[dim + 2 :])


def gather_directly(array, axis, dim):
    parts = sent_to_all(array, axis)
    return laid_out(parts, dim)


def shifted(array, axis, by):
    size = lax.axis_size(axis)
    return lax.ppermute(array, axis, [(i, (i + by) % size) for i in range(size)])


def shift_down(mixed, count):
    return lax.shift_right_logical(mixed, jnp.full(mixed.shape, count, jnp.int32))


def hashed(tile_seed, row_ids, col_ids):
    mixed = tile_seed * 374761393 + row_ids * 668265263 + col_ids * 1274126177
    mixed = mixed ^ shift_down(mixed, 15)
    mixed = mixed * 73244475
    mixed = mixed ^ shift_down(mixed, 13)
    mixed = mixed * 1911520717
    mixed = mixed ^ shift_down(mixed, 16)
    return (mixed & 65535).astype(jnp.float32) / 32768.0 - 1.0


def per_device(query_factors, panel_factors, query_weight, plan, tile_seeds):
    groups = lax.axis_size(PB)
    spread = lax.axis_size(DEV)
    position = lax.axis_index(PB)
    column = lax.axis_index(DEV)
    rows_here = query_factors.shape[0]
    cols_here = panel_factors.shape[0]
    factor_rank = query_factors.shape[1]
    u_count = float(rows_here * groups * factor_rank)
    v_count = float(cols_here * groups * spread * factor_rank)
    row_ids = position * rows_here + jnp.arange(rows_here, dtype=jnp.int32)[:, None]
    local_cols = jnp.arange(cols_here, dtype=jnp.int32)[None, :]
    factors = query_factors
    panel = panel_factors
    for stratum in range(STRATA):
        panel_id = plan[jnp.mod(position - stratum, groups)]
        tile_seed = tile_seeds[position, panel_id]
        col_ids = (panel_id * spread + column) * cols_here + local_cols
        scores = hashed(tile_seed, row_ids, col_ids)
        approx = jnp.dot(factors, panel.T, precision=lax.Precision.HIGHEST)
        weighted = query_weight[:, None] * (scores - approx)
        part_u = jnp.dot(weighted, panel, precision=lax.Precision.HIGHEST)
        grad_v = jnp.dot(weighted.T, factors, precision=lax.Precision.HIGHEST)
        norm_v = jnp.sum(grad_v * grad_v)
        share = sent_and_summed(part_u, DEV, 0)
        totals = (
            one_axis_at_a_time(jnp.sum(share * share), PB_DEV),
            one_axis_at_a_time(norm_v, PB_DEV),
        )
        step_u = learning_rate / jnp.sqrt(totals[0] / u_count + epsilon)
        share_rows = share.shape[0]
        own_rows = lax.dynamic_slice_in_dim(factors, column * share_rows, share_rows, 0)
        factors = gather_directly(own_rows + step_u * share, DEV, 0)
        step_v = learning_rate / jnp.sqrt(totals[1] / v_count + epsilon)
        panel = shifted(panel + step_v * grad_v, PB, 1)
    return (factors, panel)


def solution(mesh):
    finer = Mesh(mesh.devices.reshape(2, 8, 2, 4, 4), ("pb_0", "pb_1", "pb_2", "dev_0", "dev_1"))
    return jax.shard_map(
        per_device,
        mesh=finer,
        in_specs=(P(PB, None), P(PB_DEV, None), P(PB), P(), P()),
        out_specs=(P(PB, None), P(PB_DEV, None)),
        check_vma=False,
    )
```

profile of v0, /device:TPU:1, one launch (start us, length us, event | category | flops | bytes accessed | tf_op | source)
XLA Modules:
  0.0 292.5 jit_solution(11714593561061236251)
XLA Ops:
  0.6 0.0 copy-start.1
  0.7 1.4 fusion.25
  8.6 1.5 fusion.24
  10.0 0.0 copy-start.2
  10.7 0.0 copy-done.1
  10.7 0.0 copy-done.2
  10.7 2.3 fusion.2
  13.1 1.8 fusion.26
  14.9 0.0 copy-start
  14.9 10.5 %all-to-all-start = ((f32[16,64,128]{2,1,0:T(8,128)}), f32[16,64,128]{2,1,0:T(8,128)S(1)}, u32[]{:S(2)}, u32[]{:S(2)}) async-start(f32[16,64,128]{2,1,0:T(8,128)} %bitcast.2), calls=%async_computation | async-start | bytes 1048576 | tf_op jit(solution)/shard_map/all_to_all | solution.py:24
  25.4 0.0 copy-done
  25.4 2.4 multiply_reduce_fusion.2
  27.8 13.3 %all-to-all-done = f32[16,64,128]{2,1,0:T(8,128)S(1)} async-done(((f32[16,64,128]{2,1,0:T(8,128)}), f32[16,64,128]{2,1,0:T(8,128)S(1)}, u32[]{:S(2)}, u32[]{:S(2)}) %all-to-all-start) | async-done | bytes 524320 | tf_op jit(solution)/shard_map/all_to_all | solution.py:24
  41.1 0.6 multiply_reduce_fusion.5
  41.8 9.0 %all-reduce.14 = (f32[]{:T(128)}, f32[]{:T(128)}) all-reduce(f32[]{:T(128)} %multiply_reduce_fusion.5, f32[]{:T(128)} %get-tuple-element.38), channel_id=1, replica_groups=mesh['pb_0'=2,'pb_1'=8,'pb_2'=2,'dev_0'=4,'dev_1'=4] {'pb_0'}, use_global_device_ids=true, to_apply=%region_2.3 | all-reduce | flops 2 | bytes 16 | tf_op jit(solution)/shard_map/psum | solution.py:30
  50.8 14.5 %all-reduce.2 = (f32[]{:T(128)}, f32[]{:T(128)}) all-reduce(f32[]{:T(128)} %get-tuple-element.30, f32[]{:T(128)} %get-tuple-element.31), channel_id=1, replica_groups=mesh['pb_0'=2,'pb_1'=8,'pb_2'=2,'dev_0'=4,'dev_1'=4] {'pb_1'}, use_global_device_ids=true, to_apply=%region_3.4 | all-reduce | flops 2 | bytes 16 | tf_op jit(solution)/shard_map/psum | solution.py:30
  65.3 9.2 %all-reduce.11 = (f32[]{:T(128)}, f32[]{:T(128)}) all-reduce(f32[]{:T(128)} %get-tuple-element.6, f32[]{:T(128)} %get-tuple-element.7), channel_id=1, replica_groups=mesh['pb_0'=2,'pb_1'=8,'pb_2'=2,'dev_0'=4,'dev_1'=4] {'pb_2'}, use_global_device_ids=true, to_apply=%region_4.5 | all-reduce | flops 2 | bytes 16 | tf_op jit(solution)/shard_map/psum | solution.py:30
  74.5 7.2 %all-reduce.8 = (f32[]{:T(128)}, f32[]{:T(128)}) all-reduce(f32[]{:T(128)} %get-tuple-element.24, f32[]{:T(128)} %get-tuple-element.25), channel_id=1, replica_groups=mesh['pb_0'=2,'pb_1'=8,'pb_2'=2,'dev_0'=4,'dev_1'=4] {'dev_0'}, use_global_device_ids=true, to_apply=%region_5.6 | all-reduce | flops 2 | bytes 16 | tf_op jit(solution)/shard_map/psum | solution.py:30
  81.7 8.2 %all-reduce.5 = (f32[]{:T(128)}, f32[]{:T(128)}) all-reduce(f32[]{:T(128)} %get-tuple-element.18, f32[]{:T(128)} %get-tuple-element.19), channel_id=1, replica_groups=mesh['pb_0'=2,'pb_1'=8,'pb_2'=2,'dev_0'=4,'dev_1'=4] {'dev_1'}, use_global_device_ids=true, to_apply=%region_6.7 | all-reduce | flops 2 | bytes 16 | tf_op jit(solution)/shard_map/psum | solution.py:30
  90.6 0.8 broadcast_in_dim.6
  91.4 3.6 %all-to-all-start.1 = ((f32[16,64,128]{2,1,0:T(8,128)}), f32[16,64,128]{2,1,0:T(8,128)S(1)}, u32[]{:S(2)}, u32[]{:S(2)}) async-start(f32[16,64,128]{2,1,0:T(8,128)} %broadcast_in_dim.6), calls=%async_computation.1 | async-start | bytes 1048576 | tf_op jit(solution)/shard_map/all_to_all | solution.py:36
  96.3 6.0 %collective-permute-start = (f32[256,128]{1,0:T(8,128)S(1)}, f32[256,128]{1,0:T(8,128)S(1)}, u32[]{:S(2)}, u32[]{:S(2)}) collective-permute-start(f32[256,128]{1,0:T(8,128)S(1)} %multiply_add_fusion.2), channel_id=1, source_target_pairs={{0,16},{16,32},{32,48},{48,64},{64,80},{80,96},{96,112},{112,128},... | collective-permute-start | bytes 393224 | tf_op jit(solution)/shard_map/ppermute | solution.py:52
  102.9 1.3 collective-permute-done
  104.3 3.9 %all-to-all-done.1 = f32[16,64,128]{2,1,0:T(8,128)S(1)} async-done(((f32[16,64,128]{2,1,0:T(8,128)}), f32[16,64,128]{2,1,0:T(8,128)S(1)}, u32[]{:S(2)}, u32[]{:S(2)}) %all-to-all-start.1) | async-done | bytes 524320 | tf_op jit(solution)/shard_map/all_to_all | solution.py:36
  108.2 1.3 fusion.1
  109.5 1.8 fusion.27
  111.3 4.6 %all-to-all-start.2 = ((f32[16,64,128]{2,1,0:T(8,128)}), f32[16,64,128]{2,1,0:T(8,128)S(1)}, u32[]{:S(2)}, u32[]{:S(2)}) async-start(f32[16,64,128]{2,1,0:T(8,128)} %bitcast.6), calls=%async_computation.2 | async-start | bytes 1048576 | tf_op jit(solution)/shard_map/all_to_all | solution.py:24
  115.9 2.4 multiply_reduce_fusion.1
  118.4 8.7 %all-to-all-done.2 = f32[16,64,128]{2,1,0:T(8,128)S(1)} async-done(((f32[16,64,128]{2,1,0:T(8,128)}), f32[16,64,128]{2,1,0:T(8,128)S(1)}, u32[]{:S(2)}, u32[]{:S(2)}) %all-to-all-start.2) | async-done | bytes 524320 | tf_op jit(solution)/shard_map/all_to_all | solution.py:24
  127.1 0.6 multiply_reduce_fusion.4
  127.7 8.9 %all-reduce.13 = (f32[]{:T(128)}, f32[]{:T(128)}) all-reduce(f32[]{:T(128)} %multiply_reduce_fusion.4, f32[]{:T(128)} %get-tuple-element.40), channel_id=1, replica_groups=mesh['pb_0'=2,'pb_1'=8,'pb_2'=2,'dev_0'=4,'dev_1'=4] {'pb_0'}, use_global_device_ids=true, to_apply=%region_15.16 | all-reduce | flops 2 | bytes 16 | tf_op jit(solution)/shard_map/psum | solution.py:30
  136.6 20.6 %all-reduce.1 = (f32[]{:T(128)}, f32[]{:T(128)}) all-reduce(f32[]{:T(128)} %get-tuple-element.28, f32[]{:T(128)} %get-tuple-element.29), channel_id=1, replica_groups=mesh['pb_0'=2,'pb_1'=8,'pb_2'=2,'dev_0'=4,'dev_1'=4] {'pb_1'}, use_global_device_ids=true, to_apply=%region_16.17 | all-reduce | flops 2 | bytes 16 | tf_op jit(solution)/shard_map/psum | solution.py:30
  157.1 7.2 %all-reduce.10 = (f32[]{:T(128)}, f32[]{:T(128)}) all-reduce(f32[]{:T(128)} %get-tuple-element.4, f32[]{:T(128)} %get-tuple-element.5), channel_id=1, replica_groups=mesh['pb_0'=2,'pb_1'=8,'pb_2'=2,'dev_0'=4,'dev_1'=4] {'pb_2'}, use_global_device_ids=true, to_apply=%region_17.18 | all-reduce | flops 2 | bytes 16 | tf_op jit(solution)/shard_map/psum | solution.py:30
  164.3 7.2 %all-reduce.7 = (f32[]{:T(128)}, f32[]{:T(128)}) all-reduce(f32[]{:T(128)} %get-tuple-element.22, f32[]{:T(128)} %get-tuple-element.23), channel_id=1, replica_groups=mesh['pb_0'=2,'pb_1'=8,'pb_2'=2,'dev_0'=4,'dev_1'=4] {'dev_0'}, use_global_device_ids=true, to_apply=%region_18.19 | all-reduce | flops 2 | bytes 16 | tf_op jit(solution)/shard_map/psum | solution.py:30
  171.5 8.2 %all-reduce.4 = (f32[]{:T(128)}, f32[]{:T(128)}) all-reduce(f32[]{:T(128)} %get-tuple-element.16, f32[]{:T(128)} %get-tuple-element.17), channel_id=1, replica_groups=mesh['pb_0'=2,'pb_1'=8,'pb_2'=2,'dev_0'=4,'dev_1'=4] {'dev_1'}, use_global_device_ids=true, to_apply=%region_19.20 | all-reduce | flops 2 | bytes 16 | tf_op jit(solution)/shard_map/psum | solution.py:30
  180.4 0.8 broadcast_in_dim.7
  181.3 3.6 %all-to-all-start.3 = ((f32[16,64,128]{2,1,0:T(8,128)}), f32[16,64,128]{2,1,0:T(8,128)S(1)}, u32[]{:S(2)}, u32[]{:S(2)}) async-start(f32[16,64,128]{2,1,0:T(8,128)} %broadcast_in_dim.7), calls=%async_computation.3 | async-start | bytes 1048576 | tf_op jit(solution)/shard_map/all_to_all | solution.py:36
  186.1 8.0 %collective-permute-start.1 = (f32[256,128]{1,0:T(8,128)S(1)}, f32[256,128]{1,0:T(8,128)S(1)}, u32[]{:S(2)}, u32[]{:S(2)}) collective-permute-start(f32[256,128]{1,0:T(8,128)S(1)} %multiply_add_fusion.1), channel_id=1, source_target_pairs={{0,16},{16,32},{32,48},{48,64},{64,80},{80,96},{96,112},{112,128},... | collective-permute-start | bytes 393224 | tf_op jit(solution)/shard_map/ppermute | solution.py:52
  194.9 1.0 collective-permute-done.1
  195.9 2.1 all-to-all-done.3
  198.1 1.3 fusion
  199.4 1.8 fusion.28
  201.1 5.0 %all-to-all-start.4 = ((f32[16,64,128]{2,1,0:T(8,128)}), f32[16,64,128]{2,1,0:T(8,128)S(1)}, u32[]{:S(2)}, u32[]{:S(2)}) async-start(f32[16,64,128]{2,1,0:T(8,128)} %bitcast.10), calls=%async_computation.4 | async-start | bytes 1048576 | tf_op jit(solution)/shard_map/all_to_all | solution.py:24
  206.2 2.5 multiply_reduce_fusion
  208.7 8.7 %all-to-all-done.4 = f32[16,64,128]{2,1,0:T(8,128)S(1)} async-done(((f32[16,64,128]{2,1,0:T(8,128)}), f32[16,64,128]{2,1,0:T(8,128)S(1)}, u32[]{:S(2)}, u32[]{:S(2)}) %all-to-all-start.4) | async-done | bytes 524320 | tf_op jit(solution)/shard_map/all_to_all | solution.py:24
  217.4 0.6 multiply_reduce_fusion.3
  218.0 8.3 %all-reduce.12 = (f32[]{:T(128)}, f32[]{:T(128)}) all-reduce(f32[]{:T(128)} %multiply_reduce_fusion.3, f32[]{:T(128)} %get-tuple-element.42), channel_id=1, replica_groups=mesh['pb_0'=2,'pb_1'=8,'pb_2'=2,'dev_0'=4,'dev_1'=4] {'pb_0'}, use_global_device_ids=true, to_apply=%region_28.29 | all-reduce | flops 2 | bytes 16 | tf_op jit(solution)/shard_map/psum | solution.py:30
  226.3 21.8 %all-reduce = (f32[]{:T(128)}, f32[]{:T(128)}) all-reduce(f32[]{:T(128)} %get-tuple-element.26, f32[]{:T(128)} %get-tuple-element.27), channel_id=1, replica_groups=mesh['pb_0'=2,'pb_1'=8,'pb_2'=2,'dev_0'=4,'dev_1'=4] {'pb_1'}, use_global_device_ids=true, to_apply=%region_29.30 | all-reduce | flops 2 | bytes 16 | tf_op jit(solution)/shard_map/psum | solution.py:30
  248.1 7.5 %all-reduce.9 = (f32[]{:T(128)}, f32[]{:T(128)}) all-reduce(f32[]{:T(128)} %get-tuple-element.2, f32[]{:T(128)} %get-tuple-element.3), channel_id=1, replica_groups=mesh['pb_0'=2,'pb_1'=8,'pb_2'=2,'dev_0'=4,'dev_1'=4] {'pb_2'}, use_global_device_ids=true, to_apply=%region_30.31 | all-reduce | flops 2 | bytes 16 | tf_op jit(solution)/shard_map/psum | solution.py:30
  255.5 7.1 %all-reduce.6 = (f32[]{:T(128)}, f32[]{:T(128)}) all-reduce(f32[]{:T(128)} %get-tuple-element.20, f32[]{:T(128)} %get-tuple-element.21), channel_id=1, replica_groups=mesh['pb_0'=2,'pb_1'=8,'pb_2'=2,'dev_0'=4,'dev_1'=4] {'dev_0'}, use_global_device_ids=true, to_apply=%region_31.32 | all-reduce | flops 2 | bytes 16 | tf_op jit(solution)/shard_map/psum | solution.py:30
  262.7 9.4 %all-reduce.3 = (f32[]{:T(128)}, f32[]{:T(128)}) all-reduce(f32[]{:T(128)} %get-tuple-element.14, f32[]{:T(128)} %get-tuple-element.15), channel_id=1, replica_groups=mesh['pb_0'=2,'pb_1'=8,'pb_2'=2,'dev_0'=4,'dev_1'=4] {'dev_1'}, use_global_device_ids=true, to_apply=%region_32.33 | all-reduce | flops 2 | bytes 16 | tf_op jit(solution)/shard_map/psum | solution.py:30
  272.7 0.8 broadcast_in_dim.16
  273.6 3.6 %all-to-all-start.5 = ((f32[16,64,128]{2,1,0:T(8,128)}), f32[16,64,128]{2,1,0:T(8,128)S(1)}, u32[]{:S(2)}, u32[]{:S(2)}) async-start(f32[16,64,128]{2,1,0:T(8,128)} %broadcast_in_dim.16), calls=%async_computation.5 | async-start | bytes 1048576 | tf_op jit(solution)/shard_map/all_to_all | solution.py:36
  277.9 5.0 %collective-permute-start.2 = (f32[256,128]{1,0:T(8,128)S(1)}, f32[256,128]{1,0:T(8,128)S(1)}, u32[]{:S(2)}, u32[]{:S(2)}) collective-permute-start(f32[256,128]{1,0:T(8,128)S(1)} %multiply_add_fusion), channel_id=1, source_target_pairs={{0,16},{16,32},{32,48},{48,64},{64,80},{80,96},{96,112},{112,128},... | collective-permute-start | bytes 393224 | tf_op jit(solution)/shard_map/ppermute | solution.py:52
  282.9 1.9 collective-permute-done.2
  284.8 6.2 %all-to-all-done.5 = f32[16,64,128]{2,1,0:T(8,128)S(1)} async-done(((f32[16,64,128]{2,1,0:T(8,128)}), f32[16,64,128]{2,1,0:T(8,128)S(1)}, u32[]{:S(2)}, u32[]{:S(2)}) %all-to-all-start.5) | async-done | bytes 524320 | tf_op jit(solution)/shard_map/all_to_all | solution.py:36
  291.0 0.8 copy.9
  291.8 0.7 copy.10
  (15 shorter events, 0.2 us)
Async XLA Ops:
  0.6 10.1 %copy-start.1 = (f32[256,128]{1,0:T(8,128)S(1)}, f32[256,128]{1,0:T(8,128)}, u32[]{:S(2)}) copy-start(f32[256,128]{1,0:T(8,128)} %param.6) | copy-start | bytes 393220
  10.0 0.7 copy-start.2
  14.9 10.5 %copy-start = (f32[1024,128]{1,0:T(8,128)S(1)}, f32[1024,128]{1,0:T(8,128)}, u32[]{:S(2)}) copy-start(f32[1024,128]{1,0:T(8,128)} %param.5) | copy-start | bytes 1572868
  14.9 26.2 %all-to-all-start = ((f32[16,64,128]{2,1,0:T(8,128)}), f32[16,64,128]{2,1,0:T(8,128)S(1)}, u32[]{:S(2)}, u32[]{:S(2)}) async-start(f32[16,64,128]{2,1,0:T(8,128)} %bitcast.2), calls=%async_computation | async-start | bytes 1048576 | tf_op jit(solution)/shard_map/all_to_all | solution.py:24
  91.4 16.8 %all-to-all-start.1 = ((f32[16,64,128]{2,1,0:T(8,128)}), f32[16,64,128]{2,1,0:T(8,128)S(1)}, u32[]{:S(2)}, u32[]{:S(2)}) async-start(f32[16,64,128]{2,1,0:T(8,128)} %broadcast_in_dim.6), calls=%async_computation.1 | async-start | bytes 1048576 | tf_op jit(solution)/shard_map/all_to_all | solution.py:36
  96.3 8.0 %collective-permute-start = (f32[256,128]{1,0:T(8,128)S(1)}, f32[256,128]{1,0:T(8,128)S(1)}, u32[]{:S(2)}, u32[]{:S(2)}) collective-permute-start(f32[256,128]{1,0:T(8,128)S(1)} %multiply_add_fusion.2), channel_id=1, source_target_pairs={{0,16},{16,32},{32,48},{48,64},{64,80},{80,96},{96,112},{112,128},... | collective-permute-start | bytes 393224 | tf_op jit(solution)/shard_map/ppermute | solution.py:52
  111.3 15.8 %all-to-all-start.2 = ((f32[16,64,128]{2,1,0:T(8,128)}), f32[16,64,128]{2,1,0:T(8,128)S(1)}, u32[]{:S(2)}, u32[]{:S(2)}) async-start(f32[16,64,128]{2,1,0:T(8,128)} %bitcast.6), calls=%async_computation.2 | async-start | bytes 1048576 | tf_op jit(solution)/shard_map/all_to_all | solution.py:24
  181.3 16.8 %all-to-all-start.3 = ((f32[16,64,128]{2,1,0:T(8,128)}), f32[16,64,128]{2,1,0:T(8,128)S(1)}, u32[]{:S(2)}, u32[]{:S(2)}) async-start(f32[16,64,128]{2,1,0:T(8,128)} %broadcast_in_dim.7), calls=%async_computation.3 | async-start | bytes 1048576 | tf_op jit(solution)/shard_map/all_to_all | solution.py:36
  186.1 9.8 %collective-permute-start.1 = (f32[256,128]{1,0:T(8,128)S(1)}, f32[256,128]{1,0:T(8,128)S(1)}, u32[]{:S(2)}, u32[]{:S(2)}) collective-permute-start(f32[256,128]{1,0:T(8,128)S(1)} %multiply_add_fusion.1), channel_id=1, source_target_pairs={{0,16},{16,32},{32,48},{48,64},{64,80},{80,96},{96,112},{112,128},... | collective-permute-start | bytes 393224 | tf_op jit(solution)/shard_map/ppermute | solution.py:52
  201.1 16.2 %all-to-all-start.4 = ((f32[16,64,128]{2,1,0:T(8,128)}), f32[16,64,128]{2,1,0:T(8,128)S(1)}, u32[]{:S(2)}, u32[]{:S(2)}) async-start(f32[16,64,128]{2,1,0:T(8,128)} %bitcast.10), calls=%async_computation.4 | async-start | bytes 1048576 | tf_op jit(solution)/shard_map/all_to_all | solution.py:24
  273.6 17.5 %all-to-all-start.5 = ((f32[16,64,128]{2,1,0:T(8,128)}), f32[16,64,128]{2,1,0:T(8,128)S(1)}, u32[]{:S(2)}, u32[]{:S(2)}) async-start(f32[16,64,128]{2,1,0:T(8,128)} %broadcast_in_dim.16), calls=%async_computation.5 | async-start | bytes 1048576 | tf_op jit(solution)/shard_map/all_to_all | solution.py:36
  277.9 6.9 %collective-permute-start.2 = (f32[256,128]{1,0:T(8,128)S(1)}, f32[256,128]{1,0:T(8,128)S(1)}, u32[]{:S(2)}, u32[]{:S(2)}) collective-permute-start(f32[256,128]{1,0:T(8,128)S(1)} %multiply_add_fusion), channel_id=1, source_target_pairs={{0,16},{16,32},{32,48},{48,64},{64,80},{80,96},{96,112},{112,128},... | collective-permute-start | bytes 393224 | tf_op jit(solution)/shard_map/ppermute | solution.py:52
where the time goes:
time: 297 us; the launch traced here: 292 us
  blocking collectives  154 us (52%)
  starting transfers between devices  50 us (17%)
  waiting for transfers between devices  47.2 us (16%)
  matrix products  17.6 us (6%)
  between operations  14.7 us (5%)
  local copies, waits for them, and re-layouts  6.86 us (2%)
    psum x15, blocking collectives, one_axis_at_a_time(): array = lax.psum(array, axis)  154 us
    all_to_all x3, waiting for transfers between devices, sent_and_summed(): parts = lax.all_to_all(in_blocks(array, dim, size), axis, 0, 0, tiled=True)  30.6 us
    all_to_all x3, starting transfers between devices, sent_and_summed(): parts = lax.all_to_all(in_blocks(array, dim, size), axis, 0, 0, tiled=True)  20.2 us
    ppermute x3, starting transfers between devices, shifted(): lax.ppermute(array, axis, [(i, (i + by) % size) for i in range(size)])  19 us
    all_to_all x3, waiting for transfers between devices, sent_to_all(): return lax.all_to_all(copies, axis, split_axis=0, concat_axis=0, tiled=True)  12.2 us
    all_to_all x3, starting transfers between devices, sent_to_all(): return lax.all_to_all(copies, axis, split_axis=0, concat_axis=0, tiled=True)  10.7 us
    dot_general x3, matrix products, per_device(): grad_v = jnp.dot(weighted.T, factors, precision=lax.Precision.HIGHEST)  7.35 us
  transfers between devices with their start and end apart: 9, of which 9 were waited for; matrix products, arithmetic and copies ran while one was open for 3% of the time, Pallas kernels for 0%

commit v1 on v0

v1 whole, which is shorter than its diff:
```python
import functools

import jax
import jax.numpy as jnp
from jax import lax
from jax.experimental import pallas as pl
from jax.experimental.pallas import tpu as pltpu
from jax.sharding import Mesh
from jax.sharding import PartitionSpec as P

STRATA = 3
PB = ("zh", "y", "c")
DEV = ("x", "z")
AXES = ("zh", "y", "c", "x", "z")
EPSILON = 1e-06
RATE = 0.3
MESH = pl.DeviceIdType.MESH
F32, BF16 = jnp.float32, jnp.bfloat16
ROWS, COLS, RANK = 1024, 256, 128
GROUPS = 32
WIDTH = 16 * COLS
GROUP_ROWS, SHARE = 256, 64


def ring_hops(d, n):
    return min(d, n - d)


YC = sorted(
    [(dy, dc) for dy in range(8) for dc in range(2) if dy or dc],
    key=lambda o: -(ring_hops(o[0], 8) + 0.5 * o[1]),
)
ZX = sorted(
    [(dz, dx) for dz in range(8) for dx in range(4) if dz or dx],
    key=lambda o: -(ring_hops(o[0], 8) + ring_hops(o[1], 4)),
)


def split(value):
    high = value.astype(BF16)
    return high, (value - high.astype(F32)).astype(BF16)


def dot3(a, b, dims):
    def dot(left, right):
        return lax.dot_general(left, right, (dims, ((), ())), preferred_element_type=F32)

    return dot(a[0], b[0]) + (dot(a[0], b[1]) + dot(a[1], b[0]))


def shift_down(mixed, count):
    return lax.shift_right_logical(mixed, jnp.full(mixed.shape, count, jnp.int32))


def hashed(mixed):
    mixed = mixed ^ shift_down(mixed, 15)
    mixed = mixed * 73244475
    mixed = mixed ^ shift_down(mixed, 13)
    mixed = mixed * 1911520717
    mixed = mixed ^ shift_down(mixed, 16)
    return (mixed & 65535).astype(F32) * (1.0 / 32768.0) - 1.0


def kernel(
    u_in, v_in, w_in, plan, seeds, u_out, v_out,
    scores, u_hi, u_lo, wu_hi, wu_lo, v_hi, v_lo, d_hi, d_lo, wide,
    r_buf, rx, z_src, rz, g_full, v_next, v_got, h_src, h_got,
    n_src, n1, n2_src, n2,
    rx_s, rx_r, rz_s, rz_r, az_s, az_r, ax_s, ax_r, sh_s, sh_r, n1_s, n1_r, n2_s, n2_r,
):
    zh, y, c, x, z = (lax.axis_index(a) for a in AXES)
    place = (zh * 8 + y) * 2 + c
    ring_z = zh * 4 + z

    def place_at(by):
        other = lax.rem(place + by + GROUPS, GROUPS)
        return (other // 16, lax.rem(other // 2, 8), lax.rem(other, 2), x, z)

    def yc(offset):
        return (zh, lax.rem(y + offset[0], 8), lax.rem(c + offset[1], 2), x, z)

    def zx(offset):
        other = lax.rem(ring_z + offset[0], 8)
        return (other // 4, y, c, lax.rem(x + offset[1], 4), lax.rem(other, 4))

    def x_at(k):
        return (zh, y, c, lax.rem(x + k, 4), z)

    def z_at(j):
        return (zh, y, c, x, z ^ j)

    def send(src, dst, s_sem, r_sem, device):
        copy = pltpu.make_async_remote_copy(
            src_ref=src, dst_ref=dst, send_sem=s_sem, recv_sem=r_sem,
            device_id=device, device_id_type=MESH,
        )
        copy.start()
        return copy

    barrier = pltpu.get_barrier_semaphore()
    for offset in YC:
        pl.semaphore_signal(barrier, inc=1, device_id=yc(offset), device_id_type=MESH)
    for offset in ZX:
        pl.semaphore_signal(barrier, inc=1, device_id=zx(offset), device_id_type=MESH)
    pl.semaphore_signal(barrier, inc=1, device_id=place_at(-1), device_id_type=MESH)

    for block in range(8):
        row = jnp.broadcast_to(w_in[block : block + 1, :], (128, 128))
        wide[block * 128 : (block + 1) * 128, :] = row.T

    def fill_scores(t):
        panel = plan[lax.rem(place - t + GROUPS, GROUPS)]
        seed = seeds[place, panel]
        first_col = panel * WIDTH + (x * 4 + z) * COLS
        base = seed * 374761393 + place * (ROWS * 668265263 % 2**32 - 2**32 * (ROWS * 668265263 % 2**32 >= 2**31))
        cols = (lax.broadcasted_iota(jnp.int32, (1, COLS), 1) + first_col) * 1274126177 + base
        for block in range(16):
            rows = (lax.broadcasted_iota(jnp.int32, (64, COLS), 0) + block * 64) * 668265263
            scores[t, block * 64 : (block + 1) * 64, :] = hashed(rows + cols)

    def keep_u(value):
        u_hi[...], u_lo[...] = split(value)
        wu_hi[...], wu_lo[...] = split(value * wide[...])

    keep_u(u_in[...])
    v_hi[...], v_lo[...] = split(v_in[...])
    fill_scores(0)
    own_rows = pl.multiple_of(z * GROUP_ROWS + x * SHARE, SHARE)
    after = place_at(1)
    barrier_due = True
    v_ref = v_in

    for t in range(STRATA):
        sent_x = []
        for j in (3, 2, 1, 0):
            first = pl.multiple_of((z ^ j) * GROUP_ROWS, GROUP_ROWS)
            rows = pl.ds(first, GROUP_ROWS)
            v = (v_hi[...], v_lo[...])
            approx = dot3((u_hi[rows, :], u_lo[rows, :]), v, ((1,), (1,)))
            d = split(scores[t, rows, :] - approx)
            d_hi[rows, :], d_lo[rows, :] = d
            r_buf[t, rows, :] = dot3(d, v, ((1,), (0,)))
            if barrier_due:
                pl.semaphore_wait(barrier, len(YC) + len(ZX) + 1)
                barrier_due = False
                sent_v = send(v_in, v_got.at[0], sh_s.at[0, 0], sh_r.at[0, 0], after)
            for k in (2, 1, 3):
                part = pl.ds(pl.multiple_of(first + lax.rem(x + k, 4) * SHARE, SHARE), SHARE)
                sent_x.append(
                    send(r_buf.at[t, part], rx.at[t, j, k - 1], rx_s.at[t, j, k - 1], rx_r.at[t, j, k - 1], x_at(k))
                )
        h = dot3((d_hi[...], d_lo[...]), (wu_hi[...], wu_lo[...]), ((0,), (0,)))
        h_src[t] = h
        sent_h = send(h_src.at[t], h_got.at[t], sh_s.at[t, 1], sh_r.at[t, 1], after)
        n_src[t, 1:2, :] = jnp.sum(h * h, axis=0, keepdims=True)
        if t + 1 < STRATA:
            fill_scores(t + 1)

        sent_z = []
        for j in (3, 2, 1, 0):
            for copy in sent_x[(3 - j) * 3 : (3 - j) * 3 + 3]:
                copy.wait_recv()
            part = pl.ds(pl.multiple_of((z ^ j) * GROUP_ROWS + x * SHARE, SHARE), SHARE)
            partial = r_buf[t, part, :] + (rx[t, j, 0] + rx[t, j, 1] + rx[t, j, 2])
            if j:
                z_src[t, j - 1] = partial
                sent_z.append(
                    send(z_src.at[t, j - 1], rz.at[t, j - 1], rz_s.at[t, j - 1], rz_r.at[t, j - 1], z_at(j))
                )
        for copy in sent_z:
            copy.wait_recv()
        own = pl.ds(own_rows, SHARE)
        g = wide[own, :] * (partial + (rz[t, 0] + rz[t, 1] + rz[t, 2]))
        g_full[t, own, :] = g
        n_src[t, 0:1, :] = jnp.sum(g * g, axis=0, keepdims=True)

        sent_1 = [send(n_src.at[t], n1.at[t, i], n1_s.at[t], n1_r.at[t], yc(o)) for i, o in enumerate(YC)]
        sent_az = [
            send(g_full.at[t, own], g_full.at[t, own], az_s.at[t, j - 1], az_r.at[t, j - 1], z_at(j)) for j in (3, 2, 1)
        ]
        sent_ax = [
            send(g_full.at[t, own], g_full.at[t, own], ax_s.at[t, 0, k - 1], ax_r.at[t, 0, k - 1], x_at(k))
            for k in (2, 1, 3)
        ]

        def forward(j):
            sent_az[3 - j].wait_recv()
            part = pl.ds(pl.multiple_of((z ^ j) * GROUP_ROWS + x * SHARE, SHARE), SHARE)
            for k in (2, 1, 3):
                sent_ax.append(
                    send(g_full.at[t, part], g_full.at[t, part], ax_s.at[t, j, k - 1], ax_r.at[t, j, k - 1], x_at(k))
                )

        forward(1)
        forward(2)
        every = pltpu.make_async_remote_copy(
            src_ref=n1.at[t], dst_ref=n1.at[t], send_sem=n1_s.at[t], recv_sem=n1_r.at[t],
            device_id=after, device_id_type=MESH,
        )
        every.wait_recv()
        total = n_src[t] + jnp.sum(n1[t], axis=0)
        n2_src[t] = total
        for i, o in enumerate(ZX):
            send(n2_src.at[t], n2.at[t, i], n2_s.at[t], n2_r.at[t], zx(o))
        forward(3)
        every.wait_send()
        for copy in sent_x + sent_z + sent_az + [sent_v, sent_h]:
            copy.wait_send()
        every = pltpu.make_async_remote_copy(
            src_ref=n2.at[t], dst_ref=n2.at[t], send_sem=n2_s.at[t], recv_sem=n2_r.at[t],
            device_id=after, device_id_type=MESH,
        )
        every.wait_recv()
        total = jnp.sum(total + jnp.sum(n2[t], axis=0), axis=1, keepdims=True)
        step_u = RATE / jnp.sqrt(total[0:1] / float(ROWS * GROUPS * RANK) + EPSILON)
        step_v = RATE / jnp.sqrt(total[1:2] / float(WIDTH * GROUPS * RANK) + EPSILON)
        sent_v.wait_recv()
        sent_h.wait_recv()
        v = v_got[t] + step_v * h_got[t]
        if t + 1 < STRATA:
            v_next[t] = v
            v_hi[...], v_lo[...] = split(v)
            sent_v = send(v_next.at[t], v_got.at[t + 1], sh_s.at[t + 1, 0], sh_r.at[t + 1, 0], after)
        else:
            v_out[...] = v
        for copy in sent_ax:
            copy.wait_recv()
        u = (u_in if t == 0 else u_out)[...] + step_u * g_full[t]
        u_out[...] = u
        if t + 1 < STRATA:
            keep_u(u)
        every.wait_send()
        for copy in sent_ax:
            copy.wait_send()


def per_device(query_factors, panel_factors, query_weight, plan, tile_seeds):
    vmem = pl.BlockSpec(memory_space=pltpu.VMEM)
    smem = pl.BlockSpec(memory_space=pltpu.SMEM)
    dma = pltpu.SemaphoreType.DMA
    T = STRATA
    return pl.pallas_call(
        kernel,
        out_shape=(
            jax.ShapeDtypeStruct((ROWS, RANK), F32),
            jax.ShapeDtypeStruct((COLS, RANK), F32),
        ),
        in_specs=[vmem, vmem, vmem, smem, smem],
        out_specs=(vmem, vmem),
        scratch_shapes=[
            pltpu.VMEM((T, ROWS, COLS), F32),
            pltpu.VMEM((ROWS, RANK), BF16),
            pltpu.VMEM((ROWS, RANK), BF16),
            pltpu.VMEM((ROWS, RANK), BF16),
            pltpu.VMEM((ROWS, RANK), BF16),
            pltpu.VMEM((COLS, RANK), BF16),
            pltpu.VMEM((COLS, RANK), BF16),
            pltpu.VMEM((ROWS, COLS), BF16),
            pltpu.VMEM((ROWS, COLS), BF16),
            pltpu.VMEM((ROWS, RANK), F32),
            pltpu.VMEM((T, ROWS, RANK), F32),
            pltpu.VMEM((T, 4, 3, SHARE, RANK), F32),
            pltpu.VMEM((T, 3, SHARE, RANK), F32),
            pltpu.VMEM((T, 3, SHARE, RANK), F32),
            pltpu.VMEM((T, ROWS, RANK), F32),
            pltpu.VMEM((T, COLS, RANK), F32),
            pltpu.VMEM((T, COLS, RANK), F32),
            pltpu.VMEM((T, COLS, RANK), F32),
            pltpu.VMEM((T, COLS, RANK), F32),
            pltpu.VMEM((T, 2, RANK), F32),
            pltpu.VMEM((T, len(YC), 2, RANK), F32),
            pltpu.VMEM((T, 2, RANK), F32),
            pltpu.VMEM((T, len(ZX), 2, RANK), F32),
            dma((T, 4, 3)), dma((T, 4, 3)),
            dma((T, 3)), dma((T, 3)),
            dma((T, 3)), dma((T, 3)),
            dma((T, 4, 3)), dma((T, 4, 3)),
            dma((T, 2)), dma((T, 2)),
            dma((T,)), dma((T,)),
            dma((T,)), dma((T,)),
        ],
        compiler_params=pltpu.CompilerParams(
            collective_id=0, has_side_effects=True, vmem_limit_bytes=40 * 2**20
        ),
        name="strata",
    )(query_factors, panel_factors, query_weight.reshape(8, 128), plan, tile_seeds)


def solution(mesh):
    finer = Mesh(mesh.devices.reshape(2, 8, 2, 4, 4), AXES)
    return jax.shard_map(
        per_device,
        mesh=finer,
        in_specs=(P(PB, None), P(PB + DEV, None), P(PB), P(), P()),
        out_specs=(P(PB, None), P(PB + DEV, None)),
        check_vma=False,
    )
```

time: 297 us -> 87.9 us (0.30); the launches traced: 292 us -> 87.6 us
  blocking collectives: 154 us -> 0 us
  Pallas kernels: 0 us -> 81.5 us
  starting transfers between devices: 50 us -> 0 us
  waiting for transfers between devices: 47.2 us -> 0 us
  matrix products: 17.6 us -> 0 us
  between operations: 14.7 us -> 0.65 us
    psum x15 -> x0, blocking collectives: 154 us -> none  [one_axis_at_a_time(): array = lax.psum(array, axis)]
    pallas_call x0 -> x1, Pallas kernels: none -> 81.5 us  [per_device(): pl.pallas_call(kernel, out_shape=(jax.ShapeDtypeStruct((ROWS, RANK), F32)...]
    all_to_all x6 -> x0, waiting for transfers between devices: 42.9 us -> none  [the longest x3 30.6 us: sent_and_summed(): parts = lax.all_to_all(in_blocks(array, dim, size), axis, 0, 0, tiled=True)]
    all_to_all x6 -> x0, starting transfers between devices: 30.9 us -> none  [the longest x3 20.2 us: sent_and_summed(): parts = lax.all_to_all(in_blocks(array, dim, size), axis, 0, 0, tiled=True)]
    ppermute x3 -> x0, starting transfers between devices: 19 us -> none  [shifted(): lax.ppermute(array, axis, [(i, (i + by) % size) for i in range(size)])]
    dot_general x9 -> x0, matrix products: 17.6 us -> none  [the longest x3 7.35 us: per_device(): grad_v = jnp.dot(weighted.T, factors, precision=lax.Precision.HIGHEST)]
    ppermute x3 -> x0, waiting for transfers between devices: 4.29 us -> none  [shifted(): lax.ppermute(array, axis, [(i, (i + by) % size) for i in range(size)])]
    unnamed x8 -> x12, local copies, waits for them, and re-layouts: 1.46 us -> 5.45 us
  transfers between devices with their start and end apart: 9 -> 0, of which waited for: 9 -> 0; matrix products, arithmetic and copies ran while one was open for 3% -> 0% of each run, Pallas kernels for 0% -> 0%
where the time goes in v1:
time: 87.9 us; the launch traced here: 87.6 us
  Pallas kernels  81.5 us (93%)
  local copies, waits for them, and re-layouts  5.45 us (6%)
    pallas_call x1, Pallas kernels, per_device(): pl.pallas_call(kernel, out_shape=(jax.ShapeDtypeStruct((ROWS, RANK), F32)...  81.5 us
    unnamed x12, local copies, waits for them, and re-layouts  5.45 us

profile of v1, /device:TPU:1, one launch (start us, length us, event | category | flops | bytes accessed | tf_op | source)
XLA Modules:
  0.0 87.6 jit_solution(35227156734245462)
XLA Ops:
  0.6 0.0 copy-start.4
  0.6 0.6 copy-done.4
  1.3 0.0 copy-start
  1.3 1.0 %copy-done = f32[1024,128]{1,0:T(8,128)S(1)} copy-done((f32[1024,128]{1,0:T(8,128)S(1)}, f32[1024,128]{1,0:T(8,128)}, u32[]{:S(2)}) %copy-start) | copy-done | bytes 524312
  2.3 0.0 copy-start.1
  2.3 0.9 %copy-done.1 = f32[256,128]{1,0:T(8,128)S(1)} copy-done((f32[256,128]{1,0:T(8,128)S(1)}, f32[256,128]{1,0:T(8,128)}, u32[]{:S(2)}) %copy-start.1) | copy-done | bytes 131096
  3.2 0.0 copy-start.2
  3.2 0.7 copy-done.2
  4.0 0.0 copy-start.3
  4.0 0.7 copy-done.3
  4.6 81.5 %strata.1 = (f32[1024,128]{1,0:T(8,128)S(1)}, f32[256,128]{1,0:T(8,128)S(1)}) custom-call(f32[1024,128]{1,0:T(8,128)S(1)} %copy-done, f32[256,128]{1,0:T(8,128)S(1)} %copy-done.1, f32[8,128]{1,0:T(8,128)S(1)} %bitcast.1, s32[32]{0:T(128)S(1)} %copy-done.4, s32[32,32]{1,0:T(8,128)S(1)} %copy-done.2), custom_call_target="tpu_custom_call" | custom-call | tf_op jit(solution)/shard_map/strata/pallas_call | solution.py:242
  86.2 0.8 copy.9
  87.0 0.7 copy.10
Async XLA Ops:
  0.6 0.7 copy-start.4
  1.3 1.0 %copy-start = (f32[1024,128]{1,0:T(8,128)S(1)}, f32[1024,128]{1,0:T(8,128)}, u32[]{:S(2)}) copy-start(f32[1024,128]{1,0:T(8,128)} %u_in.1) | copy-start | bytes 1572868
  2.3 0.9 %copy-start.1 = (f32[256,128]{1,0:T(8,128)S(1)}, f32[256,128]{1,0:T(8,128)}, u32[]{:S(2)}) copy-start(f32[256,128]{1,0:T(8,128)} %v_in.1) | copy-start | bytes 393220
  3.2 0.7 copy-start.2
  4.0 0.7 copy-start.3

commit v2 on v1

v2 whole, which is shorter than its diff:
```python
import functools

import jax
import jax.numpy as jnp
from jax import lax
from jax.experimental import pallas as pl
from jax.experimental.pallas import tpu as pltpu
from jax.sharding import Mesh
from jax.sharding import PartitionSpec as P

STRATA = 3
SUMS = 3
PB = ("zh", "y", "c")
DEV = ("x", "z")
AXES = ("zh", "y", "c", "x", "z")
EPSILON = 1e-06
RATE = 0.3
MESH = pl.DeviceIdType.MESH
F32, BF16 = jnp.float32, jnp.bfloat16
ROWS, COLS, RANK = 1024, 256, 128
GROUPS = 32
WIDTH = 16 * COLS
GROUP_ROWS, SHARE = 256, 64


def ring_hops(d, n):
    return min(d, n - d)


YC = sorted(
    [(dy, dc) for dy in range(8) for dc in range(2) if dy or dc],
    key=lambda o: -(ring_hops(o[0], 8) + 0.5 * o[1]),
)
ZX = sorted(
    [(dz, dx) for dz in range(8) for dx in range(4) if dz or dx],
    key=lambda o: -(ring_hops(o[0], 8) + ring_hops(o[1], 4)),
)


def split(value):
    high = value.astype(BF16)
    return high, (value - high.astype(F32)).astype(BF16)


def dot3(a, b, dims):
    def dot(left, right):
        return lax.dot_general(left, right, (dims, ((), ())), preferred_element_type=F32)

    return dot(a[0], b[0]) + (dot(a[0], b[1]) + dot(a[1], b[0]))


def shift_down(mixed, count):
    return lax.shift_right_logical(mixed, jnp.full(mixed.shape, count, jnp.int32))


def hashed(mixed):
    mixed = mixed ^ shift_down(mixed, 15)
    mixed = mixed * 73244475
    mixed = mixed ^ shift_down(mixed, 13)
    mixed = mixed * 1911520717
    mixed = mixed ^ shift_down(mixed, 16)
    return (mixed & 65535).astype(F32) * (1.0 / 32768.0) - 1.0


def kernel(
    u_hbm, v_hbm, w_hbm, plan_hbm, seeds_hbm, u_out, v_out,
    u_now, v_now, w_in, plan, seeds,
    scores, u_hi, u_lo, wu_hi, wu_lo, v_hi, v_lo, d_hi, d_lo, wide,
    r_buf, rx, z_src, rz, g_full, v_src, v_got, h_src, h_got,
    n1_src, n1, n2_src, n2,
    in_s, rx_s, rx_r, rz_s, rz_r, az_s, az_r, ax_s, ax_r, sh_s, sh_r, n1_s, n1_r, n2_s, n2_r,
):
    zh, y, c, x, z = (lax.axis_index(a) for a in AXES)
    place = (zh * 8 + y) * 2 + c
    ring_z = zh * 4 + z

    loads = [
        pltpu.make_async_copy(src, dst, in_s.at[i])
        for i, (src, dst) in enumerate(
            [(seeds_hbm, seeds), (plan_hbm, plan), (u_hbm, u_now), (v_hbm, v_now), (w_hbm, w_in)]
        )
    ]
    for load in loads:
        load.start()

    def place_at(by):
        other = lax.rem(place + by + GROUPS, GROUPS)
        return (other // 16, lax.rem(other // 2, 8), lax.rem(other, 2), x, z)

    def yc(offset):
        return (zh, lax.rem(y + offset[0], 8), lax.rem(c + offset[1], 2), x, z)

    def zx(offset):
        other = lax.rem(ring_z + offset[0], 8)
        return (other // 4, y, c, lax.rem(x + offset[1], 4), lax.rem(other, 4))

    def x_at(k):
        return (zh, y, c, lax.rem(x + k, 4), z)

    def z_at(j):
        return (zh, y, c, x, z ^ j)

    def remote(src, dst, s_sem, r_sem, device):
        return pltpu.make_async_remote_copy(
            src_ref=src, dst_ref=dst, send_sem=s_sem, recv_sem=r_sem,
            device_id=device, device_id_type=MESH,
        )

    pending = []

    def send(src, dst, s_sem, r_sem, device):
        copy = remote(src, dst, s_sem, r_sem, device)
        copy.start()
        pending.append(copy)
        return copy

    def settle():
        for copy in pending:
            copy.wait_send()
        pending.clear()

    barrier = pltpu.get_barrier_semaphore()
    for offset in ZX:
        pl.semaphore_signal(barrier, inc=1, device_id=zx(offset), device_id_type=MESH)
    for offset in YC:
        pl.semaphore_signal(barrier, inc=1, device_id=yc(offset), device_id_type=MESH)
    pl.semaphore_signal(barrier, inc=1, device_id=place_at(-1), device_id_type=MESH)
    for load in loads:
        load.wait()

    after = place_at(1)
    own = pl.ds(pl.multiple_of(z * GROUP_ROWS + x * SHARE, SHARE), SHARE)

    def group(j):
        first = pl.multiple_of((z ^ j) * GROUP_ROWS, GROUP_ROWS)
        return first, pl.ds(first, GROUP_ROWS)

    def part(j, k=0):
        return pl.ds(
            pl.multiple_of((z ^ j) * GROUP_ROWS + lax.rem(x + k, 4) * SHARE, SHARE), SHARE
        )

    def score_base(t):
        panel = plan[lax.rem(place - t + GROUPS, GROUPS)]
        seed = seeds[place, panel]
        first_col = panel * WIDTH + (x * 4 + z) * COLS
        base = seed * 374761393 + place * ROWS * 668265263
        return (lax.broadcasted_iota(jnp.int32, (1, COLS), 1) + first_col) * 1274126177 + base

    def score_rows(cols, first, count):
        rows = (lax.broadcasted_iota(jnp.int32, (count, COLS), 0) + first) * 668265263
        return hashed(rows + cols)

    def fill_scores(t):
        cols = score_base(t)
        for block in range(16):
            scores[t - 1, block * 64 : (block + 1) * 64, :] = score_rows(cols, block * 64, 64)

    def keep_u(value):
        u_hi[...], u_lo[...] = split(value)
        wu_hi[...], wu_lo[...] = split(value * wide[...])

    def keep_v(value):
        v_hi[...], v_lo[...] = split(value)

    def v_pair():
        return v_hi[...], v_lo[...]

    def residual(rows, score):
        d = split(score - dot3((u_hi[rows, :], u_lo[rows, :]), v_pair(), ((1,), (1,))))
        d_hi[rows, :], d_lo[rows, :] = d
        return d

    def grad_v():
        return dot3((d_hi[...], d_lo[...]), (wu_hi[...], wu_lo[...]), ((0,), (0,)))

    def send_x(t, j):
        return [
            send(r_buf.at[t, part(j, k)], rx.at[t, j, k - 1], rx_s.at[t, j, k - 1], rx_r.at[t, j, k - 1], x_at(k))
            for k in (2, 1, 3)
        ]

    def collect_x(t, sent_x):
        sent_z = []
        for j in (3, 2, 1, 0):
            for copy in sent_x[j]:
                copy.wait_recv()
            partial = r_buf[t, part(j), :] + (rx[t, j, 0] + rx[t, j, 1] + rx[t, j, 2])
            if j:
                z_src[t, j - 1] = partial
                sent_z.append(
                    send(z_src.at[t, j - 1], rz.at[t, j - 1], rz_s.at[t, j - 1], rz_r.at[t, j - 1], z_at(j))
                )
        return partial, sent_z

    def collect_z(t, partial, sent_z):
        for copy in sent_z:
            copy.wait_recv()
        return partial + (rz[t, 0] + rz[t, 1] + rz[t, 2])

    def gather_z(t):
        return {
            j: send(g_full.at[t, own], g_full.at[t, own], az_s.at[t, j - 1], az_r.at[t, j - 1], z_at(j))
            for j in (3, 2, 1)
        }

    def gather_x(t):
        return [
            send(g_full.at[t, own], g_full.at[t, own], ax_s.at[t, 0, k - 1], ax_r.at[t, 0, k - 1], x_at(k))
            for k in (2, 1, 3)
        ]

    def gather_start(t):
        return gather_z(t), gather_x(t)

    def gather_forward(t, state, j):
        to_z, to_x = state
        to_z[j].wait_recv()
        for k in (2, 1, 3):
            to_x.append(
                send(
                    g_full.at[t, part(j)], g_full.at[t, part(j)],
                    ax_s.at[t, j, k - 1], ax_r.at[t, j, k - 1], x_at(k),
                )
            )

    def gather_end(t, state):
        for copy in state[1]:
            copy.wait_recv()
        return g_full[t]

    def sum_first(i):
        for slot, o in enumerate(YC):
            remote(n1_src.at[i], n1.at[i, slot], n1_s.at[i], n1_r.at[i], yc(o)).start()

    def sum_wait(i, landed, s_sem, r_sem):
        every = remote(landed.at[i], landed.at[i], s_sem.at[i], r_sem.at[i], after)
        every.wait_recv()
        pending.append(every)
        return jnp.sum(landed[i], axis=0)

    def sum_second(i):
        n2_src[i] = n1_src[i] + sum_wait(i, n1, n1_s, n1_r)
        for slot, o in enumerate(ZX):
            remote(n2_src.at[i], n2.at[i, slot], n2_s.at[i], n2_r.at[i], zx(o)).start()

    def sum_end(i):
        return jnp.sum(n2_src[i] + sum_wait(i, n2, n2_s, n2_r), axis=1, keepdims=True)

    def step_u(total):
        return RATE / jnp.sqrt(total[0:1] / float(ROWS * GROUPS * RANK) + EPSILON)

    def step_v(total):
        return RATE / jnp.sqrt(total[1:2] / float(WIDTH * GROUPS * RANK) + EPSILON)

    def squares(value):
        return jnp.sum(value * value, axis=0, keepdims=True)

    for block in range(8):
        row = jnp.broadcast_to(w_in[block : block + 1, :], (128, 128))
        wide[block * 128 : (block + 1) * 128, :] = row.T
    keep_u(u_now[...])
    keep_v(v_now[...])

    for t in range(STRATA):
        if t == 0:
            cols = score_base(0)
        else:
            sent_v = send(v_src.at[t] if t else v_now, v_got.at[t], sh_s.at[t, 0], sh_r.at[t, 0], after)
        sent_x = {}
        for j in (3, 2, 1, 0):
            first, rows = group(j)
            score = scores[t - 1, rows, :] if t else score_rows(cols, first, GROUP_ROWS)
            d = residual(rows, score)
            r_buf[t, rows, :] = dot3(d, v_pair(), ((1,), (0,)))
            if t == 0 and j == 3:
                pl.semaphore_wait(barrier, len(YC) + len(ZX) + 1)
                sent_v = send(v_now, v_got.at[0], sh_s.at[0, 0], sh_r.at[0, 0], after)
            sent_x[j] = send_x(t, j)
        h = grad_v()
        h_src[t] = h
        n1_src[t, 1:2, :] = squares(h)
        sent_h = send(h_src.at[t], h_got.at[t], sh_s.at[t, 1], sh_r.at[t, 1], after)
        if t + 1 < STRATA:
            fill_scores(t + 1)
        partial, sent_z = collect_x(t, sent_x)
        g = wide[own, :] * collect_z(t, partial, sent_z)
        g_full[t, own, :] = g
        n1_src[t, 0:1, :] = squares(g)
        sum_first(t)
        gather = gather_start(t)
        gather_forward(t, gather, 1)
        gather_forward(t, gather, 2)
        sum_second(t)
        gather_forward(t, gather, 3)
        settle()
        sent_v.wait_recv()
        sent_h.wait_recv()
        g = gather_end(t, gather)
        total = sum_end(t)
        v = v_got[t] + step_v(total) * h_got[t]
        u = u_now[...] + step_u(total) * g
        if t + 1 < STRATA:
            v_src[t + 1] = v
            keep_v(v)
            u_now[...] = u
            keep_u(u)
        else:
            v_out[...] = v
            u_out[...] = u
    settle()


def per_device(query_factors, panel_factors, query_weight, plan, tile_seeds):
    vmem = pl.BlockSpec(memory_space=pltpu.VMEM)
    anywhere = pl.BlockSpec(memory_space=pl.ANY)
    dma = pltpu.SemaphoreType.DMA
    T = STRATA
    return pl.pallas_call(
        kernel,
        out_shape=(
            jax.ShapeDtypeStruct((ROWS, RANK), F32),
            jax.ShapeDtypeStruct((COLS, RANK), F32),
        ),
        in_specs=[anywhere] * 5,
        out_specs=(vmem, vmem),
        scratch_shapes=[
            pltpu.VMEM((ROWS, RANK), F32),
            pltpu.VMEM((COLS, RANK), F32),
            pltpu.VMEM((8, RANK), F32),
            pltpu.SMEM((GROUPS,), jnp.int32),
            pltpu.SMEM((GROUPS, GROUPS), jnp.int32),
            pltpu.VMEM((T - 1, ROWS, COLS), F32),
            pltpu.VMEM((ROWS, RANK), BF16),
            pltpu.VMEM((ROWS, RANK), BF16),
            pltpu.VMEM((ROWS, RANK), BF16),
            pltpu.VMEM((ROWS, RANK), BF16),
            pltpu.VMEM((COLS, RANK), BF16),
            pltpu.VMEM((COLS, RANK), BF16),
            pltpu.VMEM((ROWS, COLS), BF16),
            pltpu.VMEM((ROWS, COLS), BF16),
            pltpu.VMEM((ROWS, RANK), F32),
            pltpu.VMEM((T, ROWS, RANK), F32),
            pltpu.VMEM((T, 4, 3, SHARE, RANK), F32),
            pltpu.VMEM((T, 3, SHARE, RANK), F32),
            pltpu.VMEM((T, 3, SHARE, RANK), F32),
            pltpu.VMEM((T, ROWS, RANK), F32),
            pltpu.VMEM((T, COLS, RANK), F32),
            pltpu.VMEM((T, COLS, RANK), F32),
            pltpu.VMEM((T, COLS, RANK), F32),
            pltpu.VMEM((T, COLS, RANK), F32),
            pltpu.VMEM((SUMS, 2, RANK), F32),
            pltpu.VMEM((SUMS, len(YC), 2, RANK), F32),
            pltpu.VMEM((SUMS, 2, RANK), F32),
            pltpu.VMEM((SUMS, len(ZX), 2, RANK), F32),
            dma((5,)),
            dma((T, 4, 3)), dma((T, 4, 3)),
            dma((T, 3)), dma((T, 3)),
            dma((T, 3)), dma((T, 3)),
            dma((T, 4, 3)), dma((T, 4, 3)),
            dma((T, 2)), dma((T, 2)),
            dma((SUMS,)), dma((SUMS,)),
            dma((SUMS,)), dma((SUMS,)),
        ],
        compiler_params=pltpu.CompilerParams(
            collective_id=0, has_side_effects=True, vmem_limit_bytes=56 * 2**20
        ),
        name="strata",
    )(query_factors, panel_factors, query_weight.reshape(8, 128), plan, tile_seeds)


def solution(mesh):
    finer = Mesh(mesh.devices.reshape(2, 8, 2, 4, 4), AXES)
    return jax.shard_map(
        per_device,
        mesh=finer,
        in_specs=(P(PB, None), P(PB + DEV, None), P(PB), P(), P()),
        out_specs=(P(PB, None), P(PB + DEV, None)),
        check_vma=False,
    )
```

time: 87.9 us -> 85.6 us (0.974)
  local copies, waits for them, and re-layouts: 5.45 us -> 2.56 us
    unnamed x12 -> x4, local copies, waits for them, and re-layouts: 5.45 us -> 2.56 us
where the time goes in v2:
time: 85.6 us; the launch traced here: 85.4 us
  Pallas kernels  82.2 us (96%)
  local copies, waits for them, and re-layouts  2.56 us (3%)
    pallas_call x1, Pallas kernels, per_device(): pl.pallas_call(kernel, out_shape=(jax.ShapeDtypeStruct((ROWS, RANK), F32)...  82.2 us
    unnamed x4, local copies, waits for them, and re-layouts  2.56 us

profile of v2, /device:TPU:1, one launch (start us, length us, event | category | flops | bytes accessed | tf_op | source)
XLA Modules:
  0.0 85.4 jit_solution(2298615039477940749)
XLA Ops:
  0.6 82.2 %strata.1 = (f32[1024,128]{1,0:T(8,128)}, f32[256,128]{1,0:T(8,128)}) custom-call(f32[1024,128]{1,0:T(8,128)} %u_hbm.1, f32[256,128]{1,0:T(8,128)} %v_hbm.1, f32[8,128]{1,0:T(8,128)} %bitcast.1, s32[32]{0:T(128)} %plan_hbm.1, s32[32,32]{1,0:T(8,128)} %seeds_hbm.1), custom_call_target="tpu_custom_call" | custom-call | tf_op jit(solution)/shard_map/strata/pallas_call | solution.py:319
  82.9 0.0 copy-start
  82.9 1.9 %copy.9 = f32[1024,128]{1,0:T(8,128)} copy(f32[1024,128]{1,0:T(8,128)} %get-tuple-element.4) | data formatting | bytes 1048576
  84.8 0.0 copy-done
  84.8 0.7 copy.10
Async XLA Ops:
  82.9 1.9 %copy-start = (f32[256,128]{1,0:T(8,128)S(1)}, f32[256,128]{1,0:T(8,128)}, u32[]{:S(2)}) copy-start(f32[256,128]{1,0:T(8,128)} %get-tuple-element.5) | copy-start | bytes 393220

commit v3 on v2

--- a/solution.py
+++ b/solution.py
@@ -156,9 +156,9 @@
         for block in range(16):
             scores[t - 1, block * 64 : (block + 1) * 64, :] = score_rows(cols, block * 64, 64)
 
-    def keep_u(value):
-        u_hi[...], u_lo[...] = split(value)
-        wu_hi[...], wu_lo[...] = split(value * wide[...])
+    def keep_u(rows, value):
+        u_hi[rows, :], u_lo[rows, :] = split(value)
+        wu_hi[rows, :], wu_lo[rows, :] = split(value * wide[rows, :])
 
     def keep_v(value):
         v_hi[...], v_lo[...] = split(value)
@@ -259,7 +259,6 @@
     for block in range(8):
         row = jnp.broadcast_to(w_in[block : block + 1, :], (128, 128))
         wide[block * 128 : (block + 1) * 128, :] = row.T
-    keep_u(u_now[...])
     keep_v(v_now[...])
 
     for t in range(STRATA):
@@ -270,6 +269,9 @@
         sent_x = {}
         for j in (3, 2, 1, 0):
             first, rows = group(j)
+            if t:
+                u_now[rows, :] = u_now[rows, :] + move * g_full[t - 1, rows, :]
+            keep_u(rows, u_now[rows, :])
             score = scores[t - 1, rows, :] if t else score_rows(cols, first, GROUP_ROWS)
             d = residual(rows, score)
             r_buf[t, rows, :] = dot3(d, v_pair(), ((1,), (0,)))
@@ -298,16 +300,14 @@
         sent_h.wait_recv()
         g = gather_end(t, gather)
         total = sum_end(t)
+        move = step_u(total)
         v = v_got[t] + step_v(total) * h_got[t]
-        u = u_now[...] + step_u(total) * g
         if t + 1 < STRATA:
             v_src[t + 1] = v
             keep_v(v)
-            u_now[...] = u
-            keep_u(u)
         else:
             v_out[...] = v
-            u_out[...] = u
+            u_out[...] = u_now[...] + move * g
     settle()
 
 

time: 85.6 us -> 85 us (level)
  no operation moved by 1% of the time
where the time goes in v3:
time: 85 us; the launch traced here: 84.8 us
  Pallas kernels  81.6 us (96%)
  local copies, waits for them, and re-layouts  2.56 us (3%)
    pallas_call x1, Pallas kernels, per_device(): pl.pallas_call(kernel, out_shape=(jax.ShapeDtypeStruct((ROWS, RANK), F32)...  81.6 us
    unnamed x4, local copies, waits for them, and re-layouts  2.56 us

profile of v3, /device:TPU:1, one launch (start us, length us, event | category | flops | bytes accessed | tf_op | source)
XLA Modules:
  0.0 84.8 jit_solution(4884462477311429919)
XLA Ops:
  0.6 81.6 %strata.1 = (f32[1024,128]{1,0:T(8,128)}, f32[256,128]{1,0:T(8,128)}) custom-call(f32[1024,128]{1,0:T(8,128)} %u_hbm.1, f32[256,128]{1,0:T(8,128)} %v_hbm.1, f32[8,128]{1,0:T(8,128)} %bitcast.1, s32[32]{0:T(128)} %plan_hbm.1, s32[32,32]{1,0:T(8,128)} %seeds_hbm.1), custom_call_target="tpu_custom_call" | custom-call | tf_op jit(solution)/shard_map/strata/pallas_call | solution.py:319
  82.2 0.0 copy-start
  82.2 1.9 %copy.9 = f32[1024,128]{1,0:T(8,128)} copy(f32[1024,128]{1,0:T(8,128)} %get-tuple-element.4) | data formatting | bytes 1048576
  84.1 0.0 copy-done
  84.1 0.7 copy.10
Async XLA Ops:
  82.2 1.9 %copy-start = (f32[256,128]{1,0:T(8,128)S(1)}, f32[256,128]{1,0:T(8,128)}, u32[]{:S(2)}) copy-start(f32[256,128]{1,0:T(8,128)} %get-tuple-element.5) | copy-start | bytes 393220

commit v4 on v3

--- a/solution.py
+++ b/solution.py
@@ -174,10 +174,10 @@
     def grad_v():
         return dot3((d_hi[...], d_lo[...]), (wu_hi[...], wu_lo[...]), ((0,), (0,)))
 
-    def send_x(t, j):
+    def send_x(t, j, peers=(2, 1, 3)):
         return [
             send(r_buf.at[t, part(j, k)], rx.at[t, j, k - 1], rx_s.at[t, j, k - 1], rx_r.at[t, j, k - 1], x_at(k))
-            for k in (2, 1, 3)
+            for k in peers
         ]
 
     def collect_x(t, sent_x):
@@ -268,17 +268,26 @@
             sent_v = send(v_src.at[t] if t else v_now, v_got.at[t], sh_s.at[t, 0], sh_r.at[t, 0], after)
         sent_x = {}
         for j in (3, 2, 1, 0):
-            first, rows = group(j)
-            if t:
-                u_now[rows, :] = u_now[rows, :] + move * g_full[t - 1, rows, :]
-            keep_u(rows, u_now[rows, :])
-            score = scores[t - 1, rows, :] if t else score_rows(cols, first, GROUP_ROWS)
-            d = residual(rows, score)
-            r_buf[t, rows, :] = dot3(d, v_pair(), ((1,), (0,)))
-            if t == 0 and j == 3:
-                pl.semaphore_wait(barrier, len(YC) + len(ZX) + 1)
-                sent_v = send(v_now, v_got.at[0], sh_s.at[0, 0], sh_r.at[0, 0], after)
-            sent_x[j] = send_x(t, j)
+            sent_x[j] = []
+            for peers in ((2,), (1,), (3,), ()) if j == 3 else ((2, 1, 3),):
+                if j == 3:
+                    first = pl.multiple_of(
+                        (z ^ j) * GROUP_ROWS + lax.rem(x + sum(peers), 4) * SHARE, SHARE
+                    )
+                    count = SHARE
+                else:
+                    first, count = group(j)[0], GROUP_ROWS
+                rows = pl.ds(first, count)
+                if t:
+                    u_now[rows, :] = u_now[rows, :] + move * g_full[t - 1, rows, :]
+                keep_u(rows, u_now[rows, :])
+                score = scores[t - 1, rows, :] if t else score_rows(cols, first, count)
+                d = residual(rows, score)
+                r_buf[t, rows, :] = dot3(d, v_pair(), ((1,), (0,)))
+                if t == 0 and peers == (2,):
+                    pl.semaphore_wait(barrier, len(YC) + len(ZX) + 1)
+                    sent_v = send(v_now, v_got.at[0], sh_s.at[0, 0], sh_r.at[0, 0], after)
+                sent_x[j] += send_x(t, j, peers)
         h = grad_v()
         h_src[t] = h
         n1_src[t, 1:2, :] = squares(h)

time: 85 us -> 86.2 us (1.014)
  Pallas kernels: 81.6 us -> 82.8 us
    pallas_call x1, Pallas kernels: 81.6 us -> 82.8 us  [per_device(): pl.pallas_call(kernel, out_shape=(jax.ShapeDtypeStruct((ROWS, RANK), F32)...]
where the time goes in v4:
time: 86.2 us; the launch traced here: 86 us
  Pallas kernels  82.8 us (96%)
  local copies, waits for them, and re-layouts  2.56 us (3%)
    pallas_call x1, Pallas kernels, per_device(): pl.pallas_call(kernel, out_shape=(jax.ShapeDtypeStruct((ROWS, RANK), F32)...  82.8 us
    unnamed x4, local copies, waits for them, and re-layouts  2.56 us

profile of v4, /device:TPU:1, one launch (start us, length us, event | category | flops | bytes accessed | tf_op | source)
XLA Modules:
  0.0 86.0 jit_solution(4152976770295807063)
XLA Ops:
  0.6 82.8 %strata.1 = (f32[1024,128]{1,0:T(8,128)}, f32[256,128]{1,0:T(8,128)}) custom-call(f32[1024,128]{1,0:T(8,128)} %u_hbm.1, f32[256,128]{1,0:T(8,128)} %v_hbm.1, f32[8,128]{1,0:T(8,128)} %bitcast.1, s32[32]{0:T(128)} %plan_hbm.1, s32[32,32]{1,0:T(8,128)} %seeds_hbm.1), custom_call_target="tpu_custom_call" | custom-call | tf_op jit(solution)/shard_map/strata/pallas_call | solution.py:328
  83.4 0.0 copy-start
  83.4 1.9 %copy.9 = f32[1024,128]{1,0:T(8,128)} copy(f32[1024,128]{1,0:T(8,128)} %get-tuple-element.4) | data formatting | bytes 1048576
  85.3 0.0 copy-done
  85.3 0.7 copy.10
Async XLA Ops:
  83.4 1.9 %copy-start = (f32[256,128]{1,0:T(8,128)S(1)}, f32[256,128]{1,0:T(8,128)}, u32[]{:S(2)}) copy-start(f32[256,128]{1,0:T(8,128)} %get-tuple-element.5) | copy-start | bytes 393220
